TPU v7x, 32 devices: a whole 2x2x4 slice. The times are simulated.
32 devices in a mesh: row: 8 (over y, x, core), col: 4 (over z).
Axes of the slice: x: 2, y: 2, z: 4, core: 2. Of those that a mesh axis runs over, the one named last changes fastest.
Arguments:
- click_tiles: bfloat16 [256, 512, 512], P(('row', 'col')), may hold values from 0 to 20
- tile_coords: int32 [256, 2], P(('row', 'col')), may hold values from 0 to 7, as said below
- tile_count: int32 [32], P(('row', 'col')), may hold values from 1 to 8, as said below
- prior_labels: float32 [64, 16384], P(None, ('row', 'col')), may hold values from 0.01 to 10
- seed_ids: int32 [1024], P(('row', 'col')), may hold values from 0 to 16383, as said below
- seed_class: int32 [1024], P(('row', 'col')), may hold values from 0 to 63
Outputs:
- query_labels: float32 [64, 16384], P(None, ('row', 'col'))
- url_labels: float32 [64, 16384], P(None, ('col', 'row'))
Inputs may be any that keep to these rules, and one draw needn't show every extreme that they name: `tile_coords`: within each device's 8 slots the (local query block, local URL block) pairs are distinct, first column below 4, second below 8. `tile_count`: some device has all 8 slots live. `seed_ids`: seeds d * 32 to (d + 1) * 32 - 1 name queries d * 512 to (d + 1) * 512 - 1.
All inputs are finite; a program needn't handle non-finite values.
Results may differ from a plain program's by a relative error of at most 0.00097.
Values may be sent and summed in bfloat16 or wider, within the bound.
A program may use at most 64 MiB of HBM per device.

v0:
```python
import jax
import jax.numpy as jnp
from jax import lax
from jax.sharding import PartitionSpec as P

BC = 8
ITERS = 2


blend_rate = 0.25
seed_weight = 8.0


def shards(click_tiles, tile_coords, tile_count, prior_labels, seed_ids, seed_class):
    col_count = lax.axis_size("col")
    row_count = lax.axis_size("row")
    slots, tile_size = (click_tiles.shape[0], click_tiles.shape[1])
    classes, query_local = prior_labels.shape
    query_slab = query_local * col_count
    query_blocks = query_slab // tile_size
    url_slab = BC * tile_size
    url_local = url_slab // row_count
    highest = lax.Precision.HIGHEST
    active = (jnp.arange(slots) < tile_count[0]).astype(jnp.float32)
    row_onehot = (tile_coords[:, 0:1] == jnp.arange(query_blocks)[None, :]).astype(
        jnp.float32
    ) * active[:, None]
    col_onehot = (tile_coords[:, 1:2] == jnp.arange(BC)[None, :]).astype(jnp.float32) * active[
        :, None
    ]
    ones_side = jnp.ones((tile_size,), jnp.bfloat16)
    row_sums = jnp.einsum("kqu,u->kq", click_tiles, ones_side, preferred_element_type=jnp.float32)
    col_sums = jnp.einsum("kqu,q->ku", click_tiles, ones_side, preferred_element_type=jnp.float32)
    query_part = jnp.einsum("kb,kq->bq", row_onehot, row_sums, precision=highest).reshape(
        query_slab
    )
    url_part = jnp.einsum("kb,ku->bu", col_onehot, col_sums, precision=highest).reshape(url_slab)
    query_deg = lax.psum_scatter(query_part, "col", scatter_dimension=0, tiled=True)
    url_deg = lax.psum_scatter(url_part, "row", scatter_dimension=0, tiled=True)
    offset = (lax.axis_index("row") * col_count + lax.axis_index("col")) * query_local
    local_ids = seed_ids - offset
    class_onehot = (seed_class[:, None] == jnp.arange(classes)[None, :]).astype(jnp.float32)
    place_onehot = (local_ids[:, None] == jnp.arange(query_local)[None, :]).astype(jnp.float32)
    seed_map = jnp.dot(class_onehot.T, place_onehot, precision=highest)
    labels = prior_labels
    url_labels = jnp.zeros((classes, url_local), jnp.float32)
    for iteration in range(ITERS):
        query_rounded = labels.astype(jnp.bfloat16)
        gathered = lax.all_gather(query_rounded, "col", axis=1, tiled=True)
        query_grid = gathered.reshape(classes, query_blocks, tile_size)
        picked = jnp.take(query_grid, tile_coords[:, 0], axis=1)
        products = jnp.einsum(
            "ckq,kqu->kcu", picked, click_tiles, preferred_element_type=jnp.float32
        )
        url_terms = jnp.einsum("kb,kcu->cbu", col_onehot, products, precision=highest).reshape(
            classes, url_slab
        )
        url_share = lax.psum_scatter(url_terms, "row", scatter_dimension=1, tiled=True)
        url_labels = url_share / (url_deg + 1.0)
        url_rounded = url_labels.astype(jnp.bfloat16)
        url_rounded_slab = lax.all_gather(url_rounded, "row", axis=1, tiled=True)
        url_grid = url_rounded_slab.reshape(classes, BC, tile_size)
        url_picked = jnp.take(url_grid, tile_coords[:, 1], axis=1)
        back = jnp.einsum(
            "cku,kqu->kcq", url_picked, click_tiles, preferred_element_type=jnp.float32
        )
        query_terms = jnp.einsum("kb,kcq->cbq", row_onehot, back, precision=highest).reshape(
            classes, query_slab
        )
        query_share = lax.psum_scatter(query_terms, "col", scatter_dimension=1, tiled=True)
        spread = query_share / (query_deg + 1.0)
        labels = (1.0 - blend_rate) * spread + blend_rate * seed_weight * seed_map
    return (labels, url_labels)


def solution(mesh):
    placed = (
        P(("row", "col"), None, None),
        P(("row", "col"), None),
        P(("row", "col")),
        P(None, ("row", "col")),
        P(("row", "col")),
        P(("row", "col")),
    )
    return jax.shard_map(
        shards,
        mesh=mesh,
        in_specs=placed,
        out_specs=(P(None, ("row", "col")), P(None, ("col", "row"))),
        check_vma=False,
    )
```

profile of v0, /device:TPU:0, one launch (start us, length us, event | category | flops | bytes accessed | tf_op | source)
XLA Modules:
  0.0 215.4 jit_solution(11458115820011137404)
XLA Ops:
  7.2 0.8 slice_bitcast_fusion.1
  8.0 0.8 compare_and_fusion
  9.4 0.9 convert_element_type.23
  10.3 15.6 %all_gather.12 = bf16[64,2048]{1,0:T(8,128)(2,1)S(1)} all-gather(bf16[64,512]{1,0:T(8,128)(2,1)S(1)} %convert_element_type.23), channel_id=1, replica_groups=mesh['row'=8,'col'=4] {'col'}, dimensions={1}, use_global_device_ids=true | all-gather | bytes 327680 | tf_op jit(solution)/shard_map/all_gather | solution.py:49
  26.6 3.1 %fusion.14 = f32[8,64,512]{2,1,0:T(8,128)S(1)} fusion(bf16[8,512,512]{2,1,0:T(8,128)(2,1)} %param.10, bf16[8,64,512]{2,1,0:T(8,128)(2,1)S(1)} %gather_fusion, pred[8]{0:T(512)(128)(4,1)S(1)} %get-tuple-element.12), kind=kOutput, calls=%fused_computation.23 | convolution fusion | flops 268697600 | bytes 5767176 | tf_op jit(solution)/shard_map/ckq,kqu->kcu/dot_general | solution.py:52
  29.7 1.7 fusion.6
  31.3 1.6 copy.31
  33.0 2.8 %fusion.47 = f32[1,8,512]{2,0,1:T(1,128)S(1)} fusion(bf16[8,512,512]{2,1,0:T(8,128)(2,1)} %param.10), kind=kOutput, calls=%fused_computation.77 | convolution fusion | flops 4194304 | bytes 4210688 | tf_op jit(solution)/shard_map/kqu,q->ku/dot_general | solution.py:33
  36.0 0.6 dynamic-slice
  37.3 22.5 %all-reduce = f32[4096]{0:T(1024)S(1)} all-reduce(f32[4096]{0:T(1024)S(1)} %bitcast.96), channel_id=3, replica_groups=mesh['row'=8,'col'=4] {'row'}, use_global_device_ids=true, to_apply=%region_1.3.clone | all-reduce | flops 4096 | bytes 32768
  59.9 10.9 %reduce-scatter.5.cloned.1.call-done = f32[64,512]{1,0:T(8,128)} async-done(((f32[64,4096]{1,0:T(8,128)}), f32[64,512]{1,0:T(8,128)}) %reduce-scatter.5.cloned.1.call-update) | async-done | bytes 131088 | tf_op jit(solution)/shard_map/reduce_scatter | solution.py:58
  70.7 0.9 divide_convert_fusion
  71.7 9.8 %all_gather.13 = bf16[64,4096]{1,0:T(8,128)(2,1)S(1)} all-gather(bf16[64,512]{1,0:T(8,128)(2,1)S(1)} %divide_convert_fusion), channel_id=1, replica_groups=mesh['row'=8,'col'=4] {'row'}, dimensions={1}, use_global_device_ids=true | all-gather | bytes 589824 | tf_op jit(solution)/shard_map/all_gather | solution.py:61
  82.1 3.6 %fusion.12 = f32[8,64,512]{2,1,0:T(8,128)S(1)} fusion(bf16[8,512,512]{2,1,0:T(8,128)(2,1)} %param.10, bf16[8,64,512]{2,1,0:T(8,128)(2,1)S(1)} %gather_fusion.1, pred[8]{0:T(512)(128)(4,1)S(1)} %get-tuple-element.6), kind=kOutput, calls=%fused_computation.21 | convolution fusion | flops 268697600 | bytes 5767176 | tf_op jit(solution)/shard_map/cku,kqu->kcq/dot_general | solution.py:64
  85.7 1.6 fusion.4
  87.3 1.0 copy.33
  89.6 3.4 %fusion.45 = f32[1,8,512]{2,0,1:T(1,128)S(1)} fusion(bf16[8,512,512]{2,1,0:T(8,128)(2,1)} %param.10), kind=kOutput, calls=%fused_computation.75 | convolution fusion | flops 4194304 | bytes 4210688 | tf_op jit(solution)/shard_map/kqu,u->kq/dot_general | solution.py:32
  93.1 12.0 %all-reduce.1 = f32[2048]{0:T(1024)S(1)} all-reduce(f32[2048]{0:T(1024)S(1)} %bitcast.97), channel_id=5, replica_groups=mesh['row'=8,'col'=4] {'col'}, use_global_device_ids=true, to_apply=%region_3.0.clone | all-reduce | flops 2048 | bytes 16384
  105.2 5.1 %reduce-scatter.7.cloned.1.call-done = f32[64,512]{1,0:T(8,128)} async-done(((f32[64,2048]{1,0:T(8,128)}), f32[64,512]{1,0:T(8,128)}) %reduce-scatter.7.cloned.1.call-update) | async-done | bytes 131088 | tf_op jit(solution)/shard_map/reduce_scatter | solution.py:70
  110.3 1.2 add_convert_fusion
  111.5 14.2 %all_gather.14 = bf16[64,2048]{1,0:T(8,128)(2,1)S(1)} all-gather(bf16[64,512]{1,0:T(8,128)(2,1)S(1)} %get-tuple-element.14), channel_id=1, replica_groups=mesh['row'=8,'col'=4] {'col'}, dimensions={1}, use_global_device_ids=true | all-gather | bytes 327680 | tf_op jit(solution)/shard_map/all_gather | solution.py:49
  126.2 3.1 %fusion.10 = f32[8,64,512]{2,1,0:T(8,128)S(1)} fusion(bf16[8,512,512]{2,1,0:T(8,128)(2,1)} %param.10, bf16[8,64,512]{2,1,0:T(8,128)(2,1)S(1)} %gather_fusion.2, pred[8]{0:T(512)(128)(4,1)S(1)} %get-tuple-element.12), kind=kOutput, calls=%fused_computation.19 | convolution fusion | flops 268697600 | bytes 5767176 | tf_op jit(solution)/shard_map/ckq,kqu->kcu/dot_general | solution.py:52
  129.3 1.7 fusion.2
  131.0 1.6 copy.35
  132.6 34.5 %reduce-scatter.9.cloned.1.call-done = f32[64,512]{1,0:T(8,128)} async-done(((f32[64,4096]{1,0:T(8,128)}), f32[64,512]{1,0:T(8,128)}) %reduce-scatter.9.cloned.1.call-update) | async-done | bytes 131088 | tf_op jit(solution)/shard_map/reduce_scatter | solution.py:58
  167.2 1.6 fusion.70
  168.7 9.9 %all_gather.15 = bf16[64,4096]{1,0:T(8,128)(2,1)S(1)} all-gather(bf16[64,512]{1,0:T(8,128)(2,1)S(1)} %get-tuple-element.4), channel_id=1, replica_groups=mesh['row'=8,'col'=4] {'row'}, dimensions={1}, use_global_device_ids=true | all-gather | bytes 589824 | tf_op jit(solution)/shard_map/all_gather | solution.py:61
  179.3 3.6 %fusion.8 = f32[8,64,512]{2,1,0:T(8,128)S(1)} fusion(bf16[8,512,512]{2,1,0:T(8,128)(2,1)} %param.10, bf16[8,64,512]{2,1,0:T(8,128)(2,1)S(1)} %gather_fusion.3, pred[8]{0:T(512)(128)(4,1)S(1)} %get-tuple-element.6), kind=kOutput, calls=%fused_computation.17 | convolution fusion | flops 268697600 | bytes 5767176 | tf_op jit(solution)/shard_map/cku,kqu->kcq/dot_general | solution.py:64
  182.9 1.6 fusion
  184.5 1.0 copy.36
  185.5 21.8 %reduce-scatter.11.cloned.1.call-done = f32[64,512]{1,0:T(8,128)} async-done(((f32[64,2048]{1,0:T(8,128)}), f32[64,512]{1,0:T(8,128)}) %reduce-scatter.11.cloned.1.call-update) | async-done | bytes 131088 | tf_op jit(solution)/shard_map/reduce_scatter | solution.py:70
  207.3 1.6 multiply_add_fusion
  (35 shorter events, 3.8 us)
Async XLA Ops:
  7.2 63.6 %reduce-scatter.5.cloned.1.call-start = ((), (), s32[]{:S(2)}) async-start(), calls=%async_computation.4 | async-start | bytes 1179648 | tf_op jit(solution)/shard_map/reduce_scatter | solution.py:58
  31.3 4.7 %copy-start.3 = (u32[32]{0:T(128)S(1)}, u32[32]{0:T(128)}, u32[]{:S(2)}) copy-start(u32[32]{0:T(128)} %constant.49) | copy-start | bytes 388
  32.9 77.3 %reduce-scatter.7.cloned.1.call-start = ((), (), s32[]{:S(2)}) async-start(), calls=%async_computation.5 | async-start | bytes 655360 | tf_op jit(solution)/shard_map/reduce_scatter | solution.py:70
  82.1 6.2 %copy-start.2 = (u32[32]{0:T(128)S(1)}, u32[32]{0:T(128)}, u32[]{:S(2)}) copy-start(u32[32]{0:T(128)} %constant.53) | copy-start | bytes 388
  85.7 19.5 %copy-start = (s32[32]{0:T(128)S(1)}, s32[32]{0:T(128)}, u32[]{:S(2)}) copy-start(s32[32]{0:T(128)} %param.14) | copy-start | bytes 388
  85.7 24.6 %copy-start.1 = (s32[32]{0:T(128)S(1)}, s32[32]{0:T(128)}, u32[]{:S(2)}) copy-start(s32[32]{0:T(128)} %param.15) | copy-start | bytes 388
  88.3 78.9 %reduce-scatter.9.cloned.1.call-start = ((), (), s32[]{:S(2)}) async-start(), calls=%async_computation.6 | async-start | bytes 1179648 | tf_op jit(solution)/shard_map/reduce_scatter | solution.py:58
  132.6 74.7 %reduce-scatter.11.cloned.1.call-start = ((), (), s32[]{:S(2)}) async-start(), calls=%async_computation.7 | async-start | bytes 655360 | tf_op jit(solution)/shard_map/reduce_scatter | solution.py:70
Sparse Core Ops, SparseCore 0:
  33.1 37.6 reduce-scatter.4
  88.4 21.8 reduce-scatter.6
  132.7 34.3 reduce-scatter.8
  185.6 21.6 reduce-scatter.10
where the time goes:
time: 216 us; the launch traced here: 215 us
  blocking collectives  84 us (39%)
  waiting for transfers between devices  72.4 us (34%)
  matrix products  27.5 us (13%)
  between operations  15.9 us (7%)
  local copies, waits for them, and re-layouts  9.48 us (4%)
  other arithmetic  5.93 us (3%)
    reduce_scatter x2, waiting for transfers between devices, shards(): lax.psum_scatter(url_terms, 'row', scatter_dimension=1, tiled=True)  45.4 us
    unnamed x2, blocking collectives  34.5 us
    all_gather x2, blocking collectives, shards(): gathered = lax.all_gather(query_rounded, 'col', axis=1, tiled=True)  29.8 us
    reduce_scatter x2, waiting for transfers between devices, shards(): lax.psum_scatter(query_terms, 'col', scatter_dimension=1, tiled=True)  27 us
    all_gather x2, blocking collectives, shards(): url_rounded_slab = lax.all_gather(url_rounded, 'row', axis=1, tiled=True)  19.7 us
    dot_general x2, matrix products, shards(): jnp.einsum('cku,kqu->kcq', url_picked, click_tiles, preferred_element_typ...  7.17 us
    unnamed x16, local copies, waits for them, and re-layouts  6.29 us
    dot_general x2, matrix products, shards(): jnp.einsum('ckq,kqu->kcu', picked, click_tiles, preferred_element_type=jn...  6.18 us
  transfers between devices with their start and end apart: 4, of which 4 were waited for; matrix products, arithmetic and copies ran while one was open for 4% of the time, Pallas kernels for 0%

commit v1 on v0

v1 whole, which is shorter than its diff:
```python
import functools

import jax
import jax.numpy as jnp
from jax import lax
from jax.experimental import pallas as pl
from jax.experimental.pallas import tpu as pltpu
from jax.sharding import PartitionSpec as P

BC = 8
ITERS = 2
GROUPS = 2

blend_rate = 0.25
seed_weight = 8.0

MESH = pl.DeviceIdType.MESH


def kernel(
    n_row, n_col,
    coords, count, prior, seed_ids, seed_class, tiles_hbm,
    labels_out, url_out,
    tiles, prods, qsend, qgrid, part, cross, summed, rowbuf, ugrid, dsend, drecv,
    udeg_part, udeg_recv, qdeg_part, qdeg_recv, udeg_inv, qdeg_inv, seeds,
    tile_sem, a_send, a_recv, b_send, b_recv, c_send, c_recv, d_send, d_recv, g_send, g_recv,
):
    slots, side = tiles.shape[0], tiles.shape[1]
    groups, members = qsend.shape[1], qsend.shape[2]
    q_local, u_local = qsend.shape[3], url_out.shape[1]
    q_blocks = qgrid[0][0].shape[0]
    chips = n_row // 2
    q_split, u_split = side // q_local, side // u_local
    row, col = lax.axis_index("row"), lax.axis_index("col")
    chip, core = row // 2, row % 2
    partner = chip * 2 + 1 - core

    def place(ref, index, split, local):
        if split == 1:
            return ref.at[index]
        start = pl.multiple_of((index % split) * local, local)
        return ref.at[index // split, :, pl.ds(start, local)]

    def copy(src, dst, send, recv, **device):
        return pltpu.make_async_remote_copy(
            src_ref=src, dst_ref=dst, send_sem=send, recv_sem=recv,
            device_id=device, device_id_type=MESH,
        )

    started = []

    def go(op):
        op.start()
        started.append(op)

    loads = [
        pltpu.make_async_copy(tiles_hbm.at[k], tiles.at[k], tile_sem.at[k]) for k in range(slots)
    ]
    for load in loads:
        load.start()

    barrier = pltpu.get_barrier_semaphore()
    for step in range(1, n_row):
        pl.semaphore_signal(
            barrier, inc=1, device_id={"row": lax.rem(row + step, n_row)}, device_id_type=MESH
        )
    for step in range(1, n_col):
        pl.semaphore_signal(
            barrier, inc=1, device_id={"col": lax.rem(col + step, n_col)}, device_id_type=MESH
        )

    def send_queries(it, g, values):
        rounded = values.astype(jnp.bfloat16)
        qsend[it, g] = rounded
        here = place(qgrid[it][g], col, q_split, q_local)
        here[...] = rounded

    def start_queries(it, g):
        for step in range(1, n_col):
            go(copy(
                qsend.at[it, g], place(qgrid[it][g], col, q_split, q_local),
                a_send.at[it, g, step], a_recv.at[it, g, step],
                col=lax.rem(col + step, n_col),
            ))

    for g in range(groups):
        send_queries(0, g, prior[g * members:(g + 1) * members, :])
    pl.semaphore_wait(barrier, n_row + n_col - 2)
    for g in range(groups):
        start_queries(0, g)

    weight = [
        [
            jnp.where((coords[k, 1] == b) & (k < count[0]), 1.0, 0.0).astype(jnp.float32)
            for k in range(slots)
        ]
        for b in range(BC)
    ]
    back_weight = [
        [
            jnp.where((coords[k, 0] == a) & (k < count[0]), 1.0, 0.0).astype(jnp.float32)
            for k in range(slots)
        ]
        for a in range(q_blocks)
    ]

    def combine(weights, values):
        total = weights[0] * values(0)
        for k in range(1, slots):
            total = total + weights[k] * values(k)
        return total

    across = (((1,), (1,)), ((), ()))

    ones = jnp.ones((16, side), jnp.bfloat16)
    for k in range(slots):
        loads[k].wait()
        down = jnp.dot(ones, tiles[k], preferred_element_type=jnp.float32)
        along = lax.dot_general(ones, tiles[k], across, preferred_element_type=jnp.float32)
        prods[k, 0:8, :] = down[0:8]
        prods[k, 8:16, :] = along[0:8]
    for b in range(BC):
        total = combine(weight[b], lambda k: prods[k, 0:8, :])
        for i in range(u_split):
            udeg_part[b * u_split + i] = total[:, i * u_local:(i + 1) * u_local]
    for a in range(q_blocks):
        total = combine(back_weight[a], lambda k: prods[k, 8:16, :])
        for i in range(q_split):
            qdeg_part[a * q_split + i] = total[:, i * q_local:(i + 1) * q_local]
    for step in range(1, n_row):
        peer = lax.rem(row + step, n_row)
        go(copy(udeg_part.at[peer], udeg_recv.at[step], g_send.at[0, step], g_recv.at[0, step], row=peer))
    for step in range(1, n_col):
        peer = lax.rem(col + step, n_col)
        go(copy(qdeg_part.at[peer], qdeg_recv.at[step], g_send.at[1, step], g_recv.at[1, step], col=peer))

    seed_count = seed_ids.shape[1]
    offset = (row * n_col + col) * q_local
    classes = groups * members
    class_hit = (
        lax.broadcasted_iota(jnp.int32, (classes, seed_count), 0) == seed_class[...]
    ).astype(jnp.float32).astype(jnp.bfloat16)
    place_hit = (
        lax.broadcasted_iota(jnp.int32, (q_local, seed_count), 0) == seed_ids[...] - offset
    ).astype(jnp.float32).astype(jnp.bfloat16)
    seeds[...] = (blend_rate * seed_weight) * lax.dot_general(
        class_hit, place_hit, across, preferred_element_type=jnp.float32
    )

    for it in range(ITERS):
        for g in range(groups):
            for step in range(1, n_col):
                copy(
                    qsend.at[it, g], place(qgrid[it][g], col, q_split, q_local),
                    a_send.at[it, g, step], a_recv.at[it, g, step], col=col,
                ).wait_recv()
            for k in range(slots):
                prods[k, 0:members, :] = jnp.dot(
                    qgrid[it][g][coords[k, 0]], tiles[k], preferred_element_type=jnp.float32
                )
            for b in range(BC):
                total = combine(weight[b], lambda k: prods[k, 0:members, :])
                for i in range(u_split):
                    owner = b * u_split + i
                    part[it, g, owner % 2, owner // 2] = total[:, i * u_local:(i + 1) * u_local]
            go(copy(
                part.at[it, g, 1 - core], cross.at[it, g], b_send.at[it, g, 0], b_recv.at[it, g, 0],
                row=partner,
            ))
        for g in range(groups):
            copy(
                part.at[it, g, 1 - core], cross.at[it, g], b_send.at[it, g, 0], b_recv.at[it, g, 0],
                row=partner,
            ).wait_recv()
            for step in list(range(1, chips)) + [0]:
                peer = lax.rem(chip + step, chips)
                summed[it, g, step] = part[it, g, core, peer] + cross[it, g, peer]
                if step:
                    go(copy(
                        summed.at[it, g, step], rowbuf.at[it, g, step],
                        b_send.at[it, g, step], b_recv.at[it, g, step], row=peer * 2 + core,
                    ))
        if it == 0:
            total = udeg_part[row]
            for step in range(1, n_row):
                copy(
                    udeg_part.at[step], udeg_recv.at[step], g_send.at[0, step], g_recv.at[0, step],
                    row=row,
                ).wait_recv()
                total = total + udeg_recv[step]
            udeg_inv[...] = 1.0 / (total + 1.0)
        for g in range(groups):
            total = summed[it, g, 0]
            for step in range(1, chips):
                copy(
                    summed.at[it, g, step], rowbuf.at[it, g, step],
                    b_send.at[it, g, step], b_recv.at[it, g, step], row=row,
                ).wait_recv()
                total = total + rowbuf[it, g, step]
            url_labels = total * udeg_inv[0:1, :]
            if it == ITERS - 1:
                url_out[g * members:(g + 1) * members, :] = url_labels
            mine = place(ugrid[it][g], row, u_split, u_local)
            mine[...] = url_labels.astype(jnp.bfloat16)
            for step in range(1, chips):
                peer = lax.rem(chip + step, chips)
                go(copy(mine, mine, c_send.at[it, g, step], c_recv.at[it, g, step], row=peer * 2 + core))
            go(copy(mine, mine, c_send.at[it, g, 0], c_recv.at[it, g, 0], row=partner))
        for g in range(groups):
            for step in range(1, chips):
                source = lax.rem(chip + chips - step, chips) * 2 + core
                piece = place(ugrid[it][g], source, u_split, u_local)
                copy(piece, piece, c_send.at[it, g, step], c_recv.at[it, g, step], row=row).wait_recv()
                go(copy(
                    piece, piece, c_send.at[it, g, chips + step], c_recv.at[it, g, chips + step],
                    row=partner,
                ))
        if it == 0:
            total = qdeg_part[col]
            for step in range(1, n_col):
                copy(
                    qdeg_part.at[step], qdeg_recv.at[step], g_send.at[1, step], g_recv.at[1, step],
                    col=col,
                ).wait_recv()
                total = total + qdeg_recv[step]
            qdeg_inv[...] = (1.0 - blend_rate) / (total + 1.0)
        for g in range(groups):
            for step in range(chips):
                source = lax.rem(chip + chips - step, chips) * 2 + 1 - core
                piece = place(ugrid[it][g], source, u_split, u_local)
                index = chips + step if step else 0
                copy(piece, piece, c_send.at[it, g, index], c_recv.at[it, g, index], row=row).wait_recv()
            for k in range(slots):
                prods[k, 0:members, :] = lax.dot_general(
                    ugrid[it][g][coords[k, 1]], tiles[k], across,
                    preferred_element_type=jnp.float32,
                )
            for a in range(q_blocks):
                total = combine(back_weight[a], lambda k: prods[k, 0:members, :])
                for i in range(q_split):
                    dsend[it, g, a * q_split + i] = total[:, i * q_local:(i + 1) * q_local]
            for step in range(1, n_col):
                peer = lax.rem(col + step, n_col)
                go(copy(
                    dsend.at[it, g, peer], drecv.at[it, g, step],
                    d_send.at[it, g, step], d_recv.at[it, g, step], col=peer,
                ))
        for g in range(groups):
            total = dsend[it, g, col]
            for step in range(1, n_col):
                copy(
                    dsend.at[it, g, step], drecv.at[it, g, step],
                    d_send.at[it, g, step], d_recv.at[it, g, step], col=col,
                ).wait_recv()
                total = total + drecv[it, g, step]
            rows = slice(g * members, (g + 1) * members)
            labels = total * qdeg_inv[0:1, :] + seeds[rows, :]
            if it == ITERS - 1:
                labels_out[rows, :] = labels
            else:
                send_queries(it + 1, g, labels)
                start_queries(it + 1, g)
    for op in started:
        op.wait_send()


def shards(click_tiles, tile_coords, tile_count, prior_labels, seed_ids, seed_class):
    n_row, n_col = lax.axis_size("row"), lax.axis_size("col")
    slots, side = click_tiles.shape[0], click_tiles.shape[1]
    classes, q_local = prior_labels.shape
    q_blocks = q_local * n_col // side
    u_local = BC * side // n_row
    groups = GROUPS
    members = classes // groups
    chips = n_row // 2
    lead = (ITERS, groups)
    f32, bf16 = jnp.float32, jnp.bfloat16
    vmem = pl.BlockSpec(memory_space=pltpu.VMEM)
    smem = pl.BlockSpec(memory_space=pltpu.SMEM)
    scratch = [
        pltpu.VMEM((slots, side, side), bf16),
        pltpu.VMEM((slots, max(members, 16), side), f32),
        pltpu.VMEM(lead + (members, q_local), bf16),
        [[pltpu.VMEM((q_blocks, members, side), bf16)] * groups] * ITERS,
        pltpu.VMEM(lead + (2, chips, members, u_local), f32),
        pltpu.VMEM(lead + (chips, members, u_local), f32),
        pltpu.VMEM(lead + (chips, members, u_local), f32),
        pltpu.VMEM(lead + (chips, members, u_local), f32),
        [[pltpu.VMEM((BC, members, side), bf16)] * groups] * ITERS,
        pltpu.VMEM(lead + (n_col, members, q_local), f32),
        pltpu.VMEM(lead + (n_col, members, q_local), f32),
        pltpu.VMEM((n_row, 8, u_local), f32),
        pltpu.VMEM((n_row, 8, u_local), f32),
        pltpu.VMEM((n_col, 8, q_local), f32),
        pltpu.VMEM((n_col, 8, q_local), f32),
        pltpu.VMEM((8, u_local), f32),
        pltpu.VMEM((8, q_local), f32),
        pltpu.VMEM((classes, q_local), f32),
        pltpu.SemaphoreType.DMA((slots,)),
        pltpu.SemaphoreType.DMA(lead + (n_col,)),
        pltpu.SemaphoreType.DMA(lead + (n_col,)),
        pltpu.SemaphoreType.DMA(lead + (chips,)),
        pltpu.SemaphoreType.DMA(lead + (chips,)),
        pltpu.SemaphoreType.DMA(lead + (2 * chips,)),
        pltpu.SemaphoreType.DMA(lead + (2 * chips,)),
        pltpu.SemaphoreType.DMA(lead + (n_col,)),
        pltpu.SemaphoreType.DMA(lead + (n_col,)),
        pltpu.SemaphoreType.DMA((2, max(n_row, n_col))),
        pltpu.SemaphoreType.DMA((2, max(n_row, n_col))),
    ]
    return pl.pallas_call(
        functools.partial(kernel, n_row, n_col),
        out_shape=(
            jax.ShapeDtypeStruct((classes, q_local), f32),
            jax.ShapeDtypeStruct((classes, u_local), f32),
        ),
        in_specs=[smem, smem, vmem, vmem, vmem, pl.BlockSpec(memory_space=pl.ANY)],
        out_specs=(vmem, vmem),
        scratch_shapes=scratch,
        compiler_params=pltpu.CompilerParams(
            collective_id=0, has_side_effects=True, vmem_limit_bytes=48 * 1024 * 1024
        ),
    )(tile_coords, tile_count, prior_labels, seed_ids[None, :], seed_class[None, :], click_tiles)


def solution(mesh):
    placed = (
        P(("row", "col"), None, None),
        P(("row", "col"), None),
        P(("row", "col")),
        P(None, ("row", "col")),
        P(("row", "col")),
        P(("row", "col")),
    )
    return jax.shard_map(
        shards,
        mesh=mesh,
        in_specs=placed,
        out_specs=(P(None, ("row", "col")), P(None, ("col", "row"))),
        check_vma=False,
    )
```

time: 216 us -> 81.7 us (0.38)
  blocking collectives: 84 us -> 0 us
  Pallas kernels: 0 us -> 73.7 us
  waiting for transfers between devices: 72.4 us -> 0 us
  matrix products: 27.5 us -> 0 us
  between operations: 15.9 us -> 1.29 us
  other arithmetic: 5.93 us -> 0 us
  local copies, waits for them, and re-layouts: 9.48 us -> 6.47 us
    pallas_call x0 -> x1, Pallas kernels: none -> 73.7 us  [shards(): pl.pallas_call(functools.partial(kernel, n_row, n_col), out_shape=(jax.Sh...]
    reduce_scatter x4 -> x0, waiting for transfers between devices: 72.3 us -> none  [the longest x2 45.4 us: shards(): lax.psum_scatter(url_terms, 'row', scatter_dimension=1, tiled=True)]
    all_gather x4 -> x0, blocking collectives: 49.5 us -> none  [the longest x2 29.8 us: shards(): gathered = lax.all_gather(query_rounded, 'col', axis=1, tiled=True)]
    unnamed x2 -> x0, blocking collectives: 34.5 us -> none
    dot_general x13 -> x0, matrix products: 27.5 us -> none  [the longest x2 7.17 us: shards(): jnp.einsum('cku,kqu->kcq', url_picked, click_tiles, preferred_element_typ...]
    convert_element_type x4 -> x0, other arithmetic: 3.42 us -> none  [the longest x2 2.5 us: shards(): url_rounded = url_labels.astype(jnp.bfloat16)]
    gather x4 -> x0, local copies, waits for them, and re-layouts: 2.32 us -> none  [the longest x2 1.16 us: shards(): url_picked = jnp.take(url_grid, tile_coords[:, 1], axis=1)]
    unnamed x16 -> x11, local copies, waits for them, and re-layouts: 6.29 us -> 6.47 us
  transfers between devices with their start and end apart: 4 -> 0, of which waited for: 4 -> 0; matrix products, arithmetic and copies ran while one was open for 4% -> 0% of each run, Pallas kernels for 0% -> 0%
where the time goes in v1:
time: 81.7 us; the launch traced here: 81.4 us
  Pallas kernels  73.7 us (90%)
  local copies, waits for them, and re-layouts  6.47 us (8%)
  between operations  1.29 us (2%)
    pallas_call x1, Pallas kernels, shards(): pl.pallas_call(functools.partial(kernel, n_row, n_col), out_shape=(jax.Sh...  73.7 us
    unnamed x11, local copies, waits for them, and re-layouts  6.47 us

profile of v1, /device:TPU:0, one launch (start us, length us, event | category | flops | bytes accessed | tf_op | source)
XLA Modules:
  0.0 81.4 jit_solution(15301983535386751176)
XLA Ops:
  1.3 0.8 copy.8.coords
  2.0 0.0 copy-start
  2.0 2.2 %copy-done = bf16[8,512,512]{2,1,0:T(8,128)(2,1)S(1)} copy-done((bf16[8,512,512]{2,1,0:T(8,128)(2,1)S(1)}, bf16[8,512,512]{2,1,0:T(8,128)(2,1)}, u32[]{:S(2)}) %copy-start) | copy-done | bytes 4194328
  4.2 0.0 copy-start.1
  4.2 0.9 %copy-done.1 = f32[64,512]{1,0:T(8,128)S(1)} copy-done((f32[64,512]{1,0:T(8,128)S(1)}, f32[64,512]{1,0:T(8,128)}, u32[]{:S(2)}) %copy-start.1) | copy-done | bytes 131096
  5.1 0.0 copy-start.2
  5.1 0.7 copy-done.2
  5.8 0.0 copy-start.3
  5.8 0.7 copy-done.3
  6.4 73.7 %shard_map.77 = (f32[64,512]{1,0:T(8,128)S(1)}, f32[64,512]{1,0:T(8,128)S(1)}) custom-call(s32[8,2]{1,0:T(8,128)S(1)} %copy.8.coords, s32[1]{0:T(128)S(6)} %copy.11.count, f32[64,512]{1,0:T(8,128)S(1)} %copy-done.1, s32[1,32]{1,0:T(1,128)S(1)} %bitcast.2, s32[1,32]{1,0:T(1,128)S(1)} %bitcast.3, bf16[8,512,512]{2,1,0:T(8,128)(2,1)S(1)} %copy-done), custom_call_target="tpu_custom_call" | custom-call | tf_op jit(solution)/shard_map/pallas_call | solution.py:311
  80.1 0.7 copy.12
  80.8 0.7 copy.13
Async XLA Ops:
  2.0 2.2 %copy-start = (bf16[8,512,512]{2,1,0:T(8,128)(2,1)S(1)}, bf16[8,512,512]{2,1,0:T(8,128)(2,1)}, u32[]{:S(2)}) copy-start(bf16[8,512,512]{2,1,0:T(8,128)(2,1)} %tiles_hbm.1) | copy-start | bytes 12582916
  4.2 0.9 %copy-start.1 = (f32[64,512]{1,0:T(8,128)S(1)}, f32[64,512]{1,0:T(8,128)}, u32[]{:S(2)}) copy-start(f32[64,512]{1,0:T(8,128)} %prior.1) | copy-start | bytes 393220
  5.1 0.7 copy-start.2
  5.8 0.7 copy-start.3

commit v2 on v1

--- a/solution.py
+++ b/solution.py
@@ -9,7 +9,8 @@
 
 BC = 8
 ITERS = 2
-GROUPS = 2
+GROUPS = 4
+SKEW = 1
 
 blend_rate = 0.25
 seed_weight = 8.0
@@ -19,10 +20,11 @@
 
 def kernel(
     n_row, n_col,
-    coords, count, prior, seed_ids, seed_class, tiles_hbm,
+    coords_hbm, count_hbm, prior_hbm, seed_ids_hbm, seed_class_hbm, tiles_hbm,
     labels_out, url_out,
     tiles, prods, qsend, qgrid, part, cross, summed, rowbuf, ugrid, dsend, drecv,
     udeg_part, udeg_recv, qdeg_part, qdeg_recv, udeg_inv, qdeg_inv, seeds,
+    coords, count, prior, seed_ids, seed_class, small_sem,
     tile_sem, a_send, a_recv, b_send, b_recv, c_send, c_recv, d_send, d_recv, g_send, g_recv,
 ):
     slots, side = tiles.shape[0], tiles.shape[1]
@@ -53,6 +55,15 @@
         op.start()
         started.append(op)
 
+    small = [
+        pltpu.make_async_copy(source, target, small_sem.at[i])
+        for i, (source, target) in enumerate((
+            (prior_hbm, prior), (coords_hbm, coords), (count_hbm, count),
+            (seed_ids_hbm, seed_ids), (seed_class_hbm, seed_class),
+        ))
+    ]
+    for load in small:
+        load.start()
     loads = [
         pltpu.make_async_copy(tiles_hbm.at[k], tiles.at[k], tile_sem.at[k]) for k in range(slots)
     ]
@@ -83,6 +94,8 @@
                 col=lax.rem(col + step, n_col),
             ))
 
+    for load in small:
+        load.wait()
     for g in range(groups):
         send_queries(0, g, prior[g * members:(g + 1) * members, :])
     pl.semaphore_wait(barrier, n_row + n_col - 2)
@@ -91,14 +104,14 @@
 
     weight = [
         [
-            jnp.where((coords[k, 1] == b) & (k < count[0]), 1.0, 0.0).astype(jnp.float32)
+            jnp.where((coords[1, k] == b) & (k < count[0, 0]), 1.0, 0.0).astype(jnp.float32)
             for k in range(slots)
         ]
         for b in range(BC)
     ]
     back_weight = [
         [
-            jnp.where((coords[k, 0] == a) & (k < count[0]), 1.0, 0.0).astype(jnp.float32)
+            jnp.where((coords[0, k] == a) & (k < count[0, 0]), 1.0, 0.0).astype(jnp.float32)
             for k in range(slots)
         ]
         for a in range(q_blocks)
@@ -123,16 +136,17 @@
         total = combine(weight[b], lambda k: prods[k, 0:8, :])
         for i in range(u_split):
             udeg_part[b * u_split + i] = total[:, i * u_local:(i + 1) * u_local]
+    qdeg_part[...] = jnp.zeros_like(qdeg_part)
     for a in range(q_blocks):
         total = combine(back_weight[a], lambda k: prods[k, 8:16, :])
         for i in range(q_split):
-            qdeg_part[a * q_split + i] = total[:, i * q_local:(i + 1) * q_local]
+            qdeg_part[pl.ds(a * q_split + i, 1), :] = total[0:1, i * q_local:(i + 1) * q_local]
     for step in range(1, n_row):
         peer = lax.rem(row + step, n_row)
         go(copy(udeg_part.at[peer], udeg_recv.at[step], g_send.at[0, step], g_recv.at[0, step], row=peer))
     for step in range(1, n_col):
         peer = lax.rem(col + step, n_col)
-        go(copy(qdeg_part.at[peer], qdeg_recv.at[step], g_send.at[1, step], g_recv.at[1, step], col=peer))
+        go(copy(qdeg_part, qdeg_recv.at[step], g_send.at[1, step], g_recv.at[1, step], col=peer))
 
     seed_count = seed_ids.shape[1]
     offset = (row * n_col + col) * q_local
@@ -147,8 +161,29 @@
         class_hit, place_hit, across, preferred_element_type=jnp.float32
     )
 
-    for it in range(ITERS):
-        for g in range(groups):
+    def finish_url_degrees():
+        total = udeg_part[row]
+        for step in range(1, n_row):
+            copy(
+                udeg_part.at[step], udeg_recv.at[step], g_send.at[0, step], g_recv.at[0, step],
+                row=row,
+            ).wait_recv()
+            total = total + udeg_recv[step]
+        udeg_inv[...] = 1.0 / (total + 1.0)
+
+    def finish_query_degrees():
+        total = qdeg_part[...]
+        for step in range(1, n_col):
+            copy(
+                qdeg_part, qdeg_recv.at[step], g_send.at[1, step], g_recv.at[1, step],
+                col=col,
+            ).wait_recv()
+            total = total + qdeg_recv[step]
+        qdeg_inv[...] = (1.0 - blend_rate) / (total + 1.0)
+
+    def flow(g):
+        for it in range(ITERS):
+            yield
             for step in range(1, n_col):
                 copy(
                     qsend.at[it, g], place(qgrid[it][g], col, q_split, q_local),
@@ -156,7 +191,7 @@
                 ).wait_recv()
             for k in range(slots):
                 prods[k, 0:members, :] = jnp.dot(
-                    qgrid[it][g][coords[k, 0]], tiles[k], preferred_element_type=jnp.float32
+                    qgrid[it][g][coords[0, k]], tiles[k], preferred_element_type=jnp.float32
                 )
             for b in range(BC):
                 total = combine(weight[b], lambda k: prods[k, 0:members, :])
@@ -167,7 +202,7 @@
                 part.at[it, g, 1 - core], cross.at[it, g], b_send.at[it, g, 0], b_recv.at[it, g, 0],
                 row=partner,
             ))
-        for g in range(groups):
+            yield
             copy(
                 part.at[it, g, 1 - core], cross.at[it, g], b_send.at[it, g, 0], b_recv.at[it, g, 0],
                 row=partner,
@@ -180,16 +215,9 @@
                         summed.at[it, g, step], rowbuf.at[it, g, step],
                         b_send.at[it, g, step], b_recv.at[it, g, step], row=peer * 2 + core,
                     ))
-        if it == 0:
-            total = udeg_part[row]
-            for step in range(1, n_row):
-                copy(
-                    udeg_part.at[step], udeg_recv.at[step], g_send.at[0, step], g_recv.at[0, step],
-                    row=row,
-                ).wait_recv()
-                total = total + udeg_recv[step]
-            udeg_inv[...] = 1.0 / (total + 1.0)
-        for g in range(groups):
+            if it == 0 and g == 0:
+                finish_url_degrees()
+            yield
             total = summed[it, g, 0]
             for step in range(1, chips):
                 copy(
@@ -206,7 +234,7 @@
                 peer = lax.rem(chip + step, chips)
                 go(copy(mine, mine, c_send.at[it, g, step], c_recv.at[it, g, step], row=peer * 2 + core))
             go(copy(mine, mine, c_send.at[it, g, 0], c_recv.at[it, g, 0], row=partner))
-        for g in range(groups):
+            yield
             for step in range(1, chips):
                 source = lax.rem(chip + chips - step, chips) * 2 + core
                 piece = place(ugrid[it][g], source, u_split, u_local)
@@ -215,16 +243,9 @@
                     piece, piece, c_send.at[it, g, chips + step], c_recv.at[it, g, chips + step],
                     row=partner,
                 ))
-        if it == 0:
-            total = qdeg_part[col]
-            for step in range(1, n_col):
-                copy(
-                    qdeg_part.at[step], qdeg_recv.at[step], g_send.at[1, step], g_recv.at[1, step],
-                    col=col,
-                ).wait_recv()
-                total = total + qdeg_recv[step]
-            qdeg_inv[...] = (1.0 - blend_rate) / (total + 1.0)
-        for g in range(groups):
+            if it == 0 and g == 0:
+                finish_query_degrees()
+            yield
             for step in range(chips):
                 source = lax.rem(chip + chips - step, chips) * 2 + 1 - core
                 piece = place(ugrid[it][g], source, u_split, u_local)
@@ -232,20 +253,22 @@
                 copy(piece, piece, c_send.at[it, g, index], c_recv.at[it, g, index], row=row).wait_recv()
             for k in range(slots):
                 prods[k, 0:members, :] = lax.dot_general(
-                    ugrid[it][g][coords[k, 1]], tiles[k], across,
+                    ugrid[it][g][coords[1, k]], tiles[k], across,
                     preferred_element_type=jnp.float32,
                 )
             for a in range(q_blocks):
                 total = combine(back_weight[a], lambda k: prods[k, 0:members, :])
                 for i in range(q_split):
-                    dsend[it, g, a * q_split + i] = total[:, i * q_local:(i + 1) * q_local]
+                    owner = a * q_split + i
+                    scaled = total[:, i * q_local:(i + 1) * q_local] * qdeg_inv[owner:owner + 1, :]
+                    dsend[it, g, owner] = scaled
             for step in range(1, n_col):
                 peer = lax.rem(col + step, n_col)
                 go(copy(
                     dsend.at[it, g, peer], drecv.at[it, g, step],
                     d_send.at[it, g, step], d_recv.at[it, g, step], col=peer,
                 ))
-        for g in range(groups):
+            yield
             total = dsend[it, g, col]
             for step in range(1, n_col):
                 copy(
@@ -254,12 +277,22 @@
                 ).wait_recv()
                 total = total + drecv[it, g, step]
             rows = slice(g * members, (g + 1) * members)
-            labels = total * qdeg_inv[0:1, :] + seeds[rows, :]
+            labels = total + seeds[rows, :]
             if it == ITERS - 1:
                 labels_out[rows, :] = labels
             else:
                 send_queries(it + 1, g, labels)
                 start_queries(it + 1, g)
+        yield
+
+    stages = 6 * ITERS
+    flows = [flow(g) for g in range(groups)]
+    for g in range(groups):
+        next(flows[g])
+    for slot in range(stages + SKEW * (groups - 1)):
+        for g in range(groups):
+            if 0 <= slot - SKEW * g < stages:
+                next(flows[g])
     for op in started:
         op.wait_send()
 
@@ -276,7 +309,6 @@
     lead = (ITERS, groups)
     f32, bf16 = jnp.float32, jnp.bfloat16
     vmem = pl.BlockSpec(memory_space=pltpu.VMEM)
-    smem = pl.BlockSpec(memory_space=pltpu.SMEM)
     scratch = [
         pltpu.VMEM((slots, side, side), bf16),
         pltpu.VMEM((slots, max(members, 16), side), f32),
@@ -291,11 +323,17 @@
         pltpu.VMEM(lead + (n_col, members, q_local), f32),
         pltpu.VMEM((n_row, 8, u_local), f32),
         pltpu.VMEM((n_row, 8, u_local), f32),
-        pltpu.VMEM((n_col, 8, q_local), f32),
-        pltpu.VMEM((n_col, 8, q_local), f32),
+        pltpu.VMEM((max(n_col, 8), q_local), f32),
+        pltpu.VMEM((n_col, max(n_col, 8), q_local), f32),
         pltpu.VMEM((8, u_local), f32),
-        pltpu.VMEM((8, q_local), f32),
+        pltpu.VMEM((max(n_col, 8), q_local), f32),
         pltpu.VMEM((classes, q_local), f32),
+        pltpu.SMEM((2, slots), jnp.int32),
+        pltpu.SMEM((1, 1), jnp.int32),
+        pltpu.VMEM((classes, q_local), f32),
+        pltpu.VMEM((1, seed_ids.shape[0]), jnp.int32),
+        pltpu.VMEM((1, seed_ids.shape[0]), jnp.int32),
+        pltpu.SemaphoreType.DMA((5,)),
         pltpu.SemaphoreType.DMA((slots,)),
         pltpu.SemaphoreType.DMA(lead + (n_col,)),
         pltpu.SemaphoreType.DMA(lead + (n_col,)),
@@ -314,13 +352,13 @@
             jax.ShapeDtypeStruct((classes, q_local), f32),
             jax.ShapeDtypeStruct((classes, u_local), f32),
         ),
-        in_specs=[smem, smem, vmem, vmem, vmem, pl.BlockSpec(memory_space=pl.ANY)],
+        in_specs=[pl.BlockSpec(memory_space=pl.ANY)] * 6,
         out_specs=(vmem, vmem),
         scratch_shapes=scratch,
         compiler_params=pltpu.CompilerParams(
-            collective_id=0, has_side_effects=True, vmem_limit_bytes=48 * 1024 * 1024
+            collective_id=0, has_side_effects=True, vmem_limit_bytes=60 * 1024 * 1024
         ),
-    )(tile_coords, tile_count, prior_labels, seed_ids[None, :], seed_class[None, :], click_tiles)
+    )(tile_coords.T, tile_count[None, :], prior_labels, seed_ids[None, :], seed_class[None, :], click_tiles)
 
 
 def solution(mesh):

time: 81.7 us -> 77.9 us (0.953)
  local copies, waits for them, and re-layouts: 6.47 us -> 3.14 us
    unnamed x11 -> x2, local copies, waits for them, and re-layouts: 6.47 us -> 3.14 us
where the time goes in v2:
time: 77.9 us; the launch traced here: 77.7 us
  Pallas kernels  73.3 us (94%)
  local copies, waits for them, and re-layouts  3.14 us (4%)
  between operations  1.28 us (2%)
    pallas_call x1, Pallas kernels, shards(): pl.pallas_call(functools.partial(kernel, n_row, n_col), out_shape=(jax.Sh...  73.3 us
    unnamed x2, local copies, waits for them, and re-layouts  3.14 us

profile of v2, /device:TPU:0, one launch (start us, length us, event | category | flops | bytes accessed | tf_op | source)
XLA Modules:
  0.0 77.7 jit_solution(10618060872570540551)
XLA Ops:
  1.3 73.3 %shard_map.77 = (f32[64,512]{1,0:T(8,128)}, f32[64,512]{1,0:T(8,128)}) custom-call(s32[2,8]{1,0:T(2,128)} %bitcast.5, s32[1,1]{1,0:T(1,128)} %bitcast.4.count_hbm, f32[64,512]{1,0:T(8,128)} %prior_hbm.1, s32[1,32]{1,0:T(1,128)} %bitcast.6, s32[1,32]{1,0:T(1,128)} %bitcast.7, bf16[8,512,512]{2,1,0:T(8,128)(2,1)} %tiles_hbm.1), custom_call_target="tpu_custom_call" | custom-call | tf_op jit(solution)/shard_map/pallas_call | solution.py:349
  74.6 1.6 %copy.11 = f32[64,512]{1,0:T(8,128)} copy(f32[64,512]{1,0:T(8,128)} %get-tuple-element.4) | data formatting | bytes 262144
  76.2 1.6 %copy.12 = f32[64,512]{1,0:T(8,128)} copy(f32[64,512]{1,0:T(8,128)} %get-tuple-element.5) | data formatting | bytes 262144

commit v3 on v2

--- a/solution.py
+++ b/solution.py
@@ -9,8 +9,7 @@
 
 BC = 8
 ITERS = 2
-GROUPS = 4
-SKEW = 1
+GROUPS = 2
 
 blend_rate = 0.25
 seed_weight = 8.0
@@ -124,29 +123,10 @@
         return total
 
     across = (((1,), (1,)), ((), ()))
-
     ones = jnp.ones((16, side), jnp.bfloat16)
-    for k in range(slots):
-        loads[k].wait()
-        down = jnp.dot(ones, tiles[k], preferred_element_type=jnp.float32)
-        along = lax.dot_general(ones, tiles[k], across, preferred_element_type=jnp.float32)
-        prods[k, 0:8, :] = down[0:8]
-        prods[k, 8:16, :] = along[0:8]
-    for b in range(BC):
-        total = combine(weight[b], lambda k: prods[k, 0:8, :])
-        for i in range(u_split):
-            udeg_part[b * u_split + i] = total[:, i * u_local:(i + 1) * u_local]
-    qdeg_part[...] = jnp.zeros_like(qdeg_part)
-    for a in range(q_blocks):
-        total = combine(back_weight[a], lambda k: prods[k, 8:16, :])
-        for i in range(q_split):
-            qdeg_part[pl.ds(a * q_split + i, 1), :] = total[0:1, i * q_local:(i + 1) * q_local]
-    for step in range(1, n_row):
-        peer = lax.rem(row + step, n_row)
-        go(copy(udeg_part.at[peer], udeg_recv.at[step], g_send.at[0, step], g_recv.at[0, step], row=peer))
-    for step in range(1, n_col):
-        peer = lax.rem(col + step, n_col)
-        go(copy(qdeg_part, qdeg_recv.at[step], g_send.at[1, step], g_recv.at[1, step], col=peer))
+
+    def lead_rows(it, g, value):
+        return jnp.concatenate([value, ones], axis=0) if it == 0 and g == 0 else value
 
     seed_count = seed_ids.shape[1]
     offset = (row * n_col + col) * q_local
@@ -172,10 +152,10 @@
         udeg_inv[...] = 1.0 / (total + 1.0)
 
     def finish_query_degrees():
-        total = qdeg_part[...]
+        total = qdeg_part[col]
         for step in range(1, n_col):
             copy(
-                qdeg_part, qdeg_recv.at[step], g_send.at[1, step], g_recv.at[1, step],
+                qdeg_part.at[step], qdeg_recv.at[step], g_send.at[1, step], g_recv.at[1, step],
                 col=col,
             ).wait_recv()
             total = total + qdeg_recv[step]
@@ -190,9 +170,13 @@
                     a_send.at[it, g, step], a_recv.at[it, g, step], col=col,
                 ).wait_recv()
             for k in range(slots):
-                prods[k, 0:members, :] = jnp.dot(
-                    qgrid[it][g][coords[0, k]], tiles[k], preferred_element_type=jnp.float32
+                if it == 0 and g == 0:
+                    loads[k].wait()
+                product = jnp.dot(
+                    lead_rows(it, g, qgrid[it][g][coords[0, k]]), tiles[k],
+                    preferred_element_type=jnp.float32,
                 )
+                prods[k, 0:product.shape[0], :] = product
             for b in range(BC):
                 total = combine(weight[b], lambda k: prods[k, 0:members, :])
                 for i in range(u_split):
@@ -202,6 +186,17 @@
                 part.at[it, g, 1 - core], cross.at[it, g], b_send.at[it, g, 0], b_recv.at[it, g, 0],
                 row=partner,
             ))
+            if it == 0 and g == 0:
+                for b in range(BC):
+                    total = combine(weight[b], lambda k: prods[k, members:members + 8, :])
+                    for i in range(u_split):
+                        udeg_part[b * u_split + i] = total[:, i * u_local:(i + 1) * u_local]
+                for step in range(1, n_row):
+                    peer = lax.rem(row + step, n_row)
+                    go(copy(
+                        udeg_part.at[peer], udeg_recv.at[step],
+                        g_send.at[0, step], g_recv.at[0, step], row=peer,
+                    ))
             yield
             copy(
                 part.at[it, g, 1 - core], cross.at[it, g], b_send.at[it, g, 0], b_recv.at[it, g, 0],
@@ -215,9 +210,9 @@
                         summed.at[it, g, step], rowbuf.at[it, g, step],
                         b_send.at[it, g, step], b_recv.at[it, g, step], row=peer * 2 + core,
                     ))
+            yield
             if it == 0 and g == 0:
                 finish_url_degrees()
-            yield
             total = summed[it, g, 0]
             for step in range(1, chips):
                 copy(
@@ -243,8 +238,6 @@
                     piece, piece, c_send.at[it, g, chips + step], c_recv.at[it, g, chips + step],
                     row=partner,
                 ))
-            if it == 0 and g == 0:
-                finish_query_degrees()
             yield
             for step in range(chips):
                 source = lax.rem(chip + chips - step, chips) * 2 + 1 - core
@@ -252,23 +245,36 @@
                 index = chips + step if step else 0
                 copy(piece, piece, c_send.at[it, g, index], c_recv.at[it, g, index], row=row).wait_recv()
             for k in range(slots):
-                prods[k, 0:members, :] = lax.dot_general(
-                    ugrid[it][g][coords[1, k]], tiles[k], across,
+                product = lax.dot_general(
+                    lead_rows(it, g, ugrid[it][g][coords[1, k]]), tiles[k], across,
                     preferred_element_type=jnp.float32,
                 )
+                prods[k, 0:product.shape[0], :] = product
             for a in range(q_blocks):
                 total = combine(back_weight[a], lambda k: prods[k, 0:members, :])
                 for i in range(q_split):
                     owner = a * q_split + i
-                    scaled = total[:, i * q_local:(i + 1) * q_local] * qdeg_inv[owner:owner + 1, :]
-                    dsend[it, g, owner] = scaled
+                    dsend[it, g, owner] = total[:, i * q_local:(i + 1) * q_local]
             for step in range(1, n_col):
                 peer = lax.rem(col + step, n_col)
                 go(copy(
                     dsend.at[it, g, peer], drecv.at[it, g, step],
                     d_send.at[it, g, step], d_recv.at[it, g, step], col=peer,
                 ))
-            yield
+            if it == 0 and g == 0:
+                for a in range(q_blocks):
+                    total = combine(back_weight[a], lambda k: prods[k, members:members + 8, :])
+                    for i in range(q_split):
+                        qdeg_part[a * q_split + i] = total[:, i * q_local:(i + 1) * q_local]
+                for step in range(1, n_col):
+                    peer = lax.rem(col + step, n_col)
+                    go(copy(
+                        qdeg_part.at[peer], qdeg_recv.at[step],
+                        g_send.at[1, step], g_recv.at[1, step], col=peer,
+                    ))
+            yield
+            if it == 0 and g == 0:
+                finish_query_degrees()
             total = dsend[it, g, col]
             for step in range(1, n_col):
                 copy(
@@ -277,7 +283,7 @@
                 ).wait_recv()
                 total = total + drecv[it, g, step]
             rows = slice(g * members, (g + 1) * members)
-            labels = total + seeds[rows, :]
+            labels = total * qdeg_inv[0:1, :] + seeds[rows, :]
             if it == ITERS - 1:
                 labels_out[rows, :] = labels
             else:
@@ -285,14 +291,14 @@
                 start_queries(it + 1, g)
         yield
 
-    stages = 6 * ITERS
     flows = [flow(g) for g in range(groups)]
     for g in range(groups):
         next(flows[g])
-    for slot in range(stages + SKEW * (groups - 1)):
-        for g in range(groups):
-            if 0 <= slot - SKEW * g < stages:
-                next(flows[g])
+    for it in range(ITERS):
+        for stages in ((0,), (1,), (2,), (3, 4), (5,)):
+            for g in range(groups):
+                for stage in stages:
+                    next(flows[g])
     for op in started:
         op.wait_send()
 
@@ -311,7 +317,7 @@
     vmem = pl.BlockSpec(memory_space=pltpu.VMEM)
     scratch = [
         pltpu.VMEM((slots, side, side), bf16),
-        pltpu.VMEM((slots, max(members, 16), side), f32),
+        pltpu.VMEM((slots, members + 16, side), f32),
         pltpu.VMEM(lead + (members, q_local), bf16),
         [[pltpu.VMEM((q_blocks, members, side), bf16)] * groups] * ITERS,
         pltpu.VMEM(lead + (2, chips, members, u_local), f32),
@@ -323,10 +329,10 @@
         pltpu.VMEM(lead + (n_col, members, q_local), f32),
         pltpu.VMEM((n_row, 8, u_local), f32),
         pltpu.VMEM((n_row, 8, u_local), f32),
-        pltpu.VMEM((max(n_col, 8), q_local), f32),
-        pltpu.VMEM((n_col, max(n_col, 8), q_local), f32),
+        pltpu.VMEM((n_col, 8, q_local), f32),
+        pltpu.VMEM((n_col, 8, q_local), f32),
         pltpu.VMEM((8, u_local), f32),
-        pltpu.VMEM((max(n_col, 8), q_local), f32),
+        pltpu.VMEM((8, q_local), f32),
         pltpu.VMEM((classes, q_local), f32),
         pltpu.SMEM((2, slots), jnp.int32),
         pltpu.SMEM((1, 1), jnp.int32),
@@ -356,7 +362,7 @@
         out_specs=(vmem, vmem),
         scratch_shapes=scratch,
         compiler_params=pltpu.CompilerParams(
-            collective_id=0, has_side_effects=True, vmem_limit_bytes=60 * 1024 * 1024
+            collective_id=0, has_side_effects=True, vmem_limit_bytes=58 * 1024 * 1024
         ),
     )(tile_coords.T, tile_count[None, :], prior_labels, seed_ids[None, :], seed_class[None, :], click_tiles)
 

time: 77.9 us -> 79.3 us (1.018)
  Pallas kernels: 73.3 us -> 74.7 us
    pallas_call x1, Pallas kernels: 73.3 us -> 74.7 us  [shards(): pl.pallas_call(functools.partial(kernel, n_row, n_col), out_shape=(jax.Sh...]
where the time goes in v3:
time: 79.3 us; the launch traced here: 79.1 us
  Pallas kernels  74.7 us (94%)
  local copies, waits for them, and re-layouts  3.14 us (4%)
  between operations  1.28 us (2%)
    pallas_call x1, Pallas kernels, shards(): pl.pallas_call(functools.partial(kernel, n_row, n_col), out_shape=(jax.Sh...  74.7 us
    unnamed x2, local copies, waits for them, and re-layouts  3.14 us

profile of v3, /device:TPU:0, one launch (start us, length us, event | category | flops | bytes accessed | tf_op | source)
XLA Modules:
  0.0 79.1 jit_solution(13924180206049477499)
XLA Ops:
  1.3 74.7 %shard_map.77 = (f32[64,512]{1,0:T(8,128)}, f32[64,512]{1,0:T(8,128)}) custom-call(s32[2,8]{1,0:T(2,128)} %bitcast.5, s32[1,1]{1,0:T(1,128)} %bitcast.4.count_hbm, f32[64,512]{1,0:T(8,128)} %prior_hbm.1, s32[1,32]{1,0:T(1,128)} %bitcast.6, s32[1,32]{1,0:T(1,128)} %bitcast.7, bf16[8,512,512]{2,1,0:T(8,128)(2,1)} %tiles_hbm.1), custom_call_target="tpu_custom_call" | custom-call | tf_op jit(solution)/shard_map/pallas_call | solution.py:355
  76.0 1.6 %copy.11 = f32[64,512]{1,0:T(8,128)} copy(f32[64,512]{1,0:T(8,128)} %get-tuple-element.4) | data formatting | bytes 262144
  77.5 1.6 %copy.12 = f32[64,512]{1,0:T(8,128)} copy(f32[64,512]{1,0:T(8,128)} %get-tuple-element.5) | data formatting | bytes 262144

commit v4 on v2

--- a/solution.py
+++ b/solution.py
@@ -9,20 +9,39 @@
 
 BC = 8
 ITERS = 2
-GROUPS = 4
-SKEW = 1
+GROUPS = 2
+WIRE_TOP = 32767.0
+SCALE_LANES = 128
+SCALE_STEPS = 256.0
 
 blend_rate = 0.25
 seed_weight = 8.0
 
 MESH = pl.DeviceIdType.MESH
+
+
+def encode(ref, values):
+    top = jnp.maximum(jnp.max(values, axis=1, keepdims=True), 1e-30)
+    power = jnp.floor(jnp.log2(top) * SCALE_STEPS) + 2.0
+    steps = values * (WIRE_TOP * jnp.exp2(power * (-1.0 / SCALE_STEPS))) + 0.5
+    width = values.shape[1]
+    ref[:, 0:width] = steps.astype(jnp.int32).astype(jnp.int16)
+    ref[:, width:width + SCALE_LANES] = jnp.broadcast_to(
+        power, (values.shape[0], SCALE_LANES)
+    ).astype(jnp.int32).astype(jnp.int16)
+
+
+def decode(ref, width):
+    power = ref[:, width:width + SCALE_LANES].astype(jnp.int32).astype(jnp.float32)
+    unit = jnp.exp2(power * (1.0 / SCALE_STEPS)) * (1.0 / WIRE_TOP)
+    return ref[:, 0:width].astype(jnp.int32).astype(jnp.float32) * unit[:, 0:1]
 
 
 def kernel(
     n_row, n_col,
     coords_hbm, count_hbm, prior_hbm, seed_ids_hbm, seed_class_hbm, tiles_hbm,
     labels_out, url_out,
-    tiles, prods, qsend, qgrid, part, cross, summed, rowbuf, ugrid, dsend, drecv,
+    tiles, prods, qsend, qgrid, part, cross, summed, rowbuf, own, ugrid, dsend, dcode, drecv,
     udeg_part, udeg_recv, qdeg_part, qdeg_recv, udeg_inv, qdeg_inv, seeds,
     coords, count, prior, seed_ids, seed_class, small_sem,
     tile_sem, a_send, a_recv, b_send, b_recv, c_send, c_recv, d_send, d_recv, g_send, g_recv,
@@ -135,7 +154,7 @@
     for b in range(BC):
         total = combine(weight[b], lambda k: prods[k, 0:8, :])
         for i in range(u_split):
-            udeg_part[b * u_split + i] = total[:, i * u_local:(i + 1) * u_local]
+            udeg_part[pl.ds(b * u_split + i, 1), :] = total[0:1, i * u_local:(i + 1) * u_local]
     qdeg_part[...] = jnp.zeros_like(qdeg_part)
     for a in range(q_blocks):
         total = combine(back_weight[a], lambda k: prods[k, 8:16, :])
@@ -143,7 +162,7 @@
             qdeg_part[pl.ds(a * q_split + i, 1), :] = total[0:1, i * q_local:(i + 1) * q_local]
     for step in range(1, n_row):
         peer = lax.rem(row + step, n_row)
-        go(copy(udeg_part.at[peer], udeg_recv.at[step], g_send.at[0, step], g_recv.at[0, step], row=peer))
+        go(copy(udeg_part, udeg_recv.at[step], g_send.at[0, step], g_recv.at[0, step], row=peer))
     for step in range(1, n_col):
         peer = lax.rem(col + step, n_col)
         go(copy(qdeg_part, qdeg_recv.at[step], g_send.at[1, step], g_recv.at[1, step], col=peer))
@@ -162,14 +181,16 @@
     )
 
     def finish_url_degrees():
-        total = udeg_part[row]
+        total = udeg_part[...]
         for step in range(1, n_row):
             copy(
-                udeg_part.at[step], udeg_recv.at[step], g_send.at[0, step], g_recv.at[0, step],
+                udeg_part, udeg_recv.at[step], g_send.at[0, step], g_recv.at[0, step],
                 row=row,
             ).wait_recv()
             total = total + udeg_recv[step]
-        udeg_inv[...] = 1.0 / (total + 1.0)
+        inverse = 1.0 / (total + 1.0)
+        for owner in range(n_row):
+            udeg_inv[owner] = jnp.broadcast_to(inverse[owner:owner + 1, :], (8, u_local))
 
     def finish_query_degrees():
         total = qdeg_part[...]
@@ -207,25 +228,29 @@
                 part.at[it, g, 1 - core], cross.at[it, g], b_send.at[it, g, 0], b_recv.at[it, g, 0],
                 row=partner,
             ).wait_recv()
+            if it == 0 and g == 0:
+                finish_url_degrees()
             for step in list(range(1, chips)) + [0]:
                 peer = lax.rem(chip + step, chips)
-                summed[it, g, step] = part[it, g, core, peer] + cross[it, g, peer]
-                if step:
+                both = part[it, g, core, peer] + cross[it, g, peer]
+                both = both * udeg_inv[peer * 2 + core][0:1, :]
+                if step == 0:
+                    own[it, g] = both
+                else:
+                    encode(summed.at[it, g, step], both)
                     go(copy(
                         summed.at[it, g, step], rowbuf.at[it, g, step],
                         b_send.at[it, g, step], b_recv.at[it, g, step], row=peer * 2 + core,
                     ))
-            if it == 0 and g == 0:
-                finish_url_degrees()
-            yield
-            total = summed[it, g, 0]
+            yield
+            total = own[it, g]
             for step in range(1, chips):
                 copy(
                     summed.at[it, g, step], rowbuf.at[it, g, step],
                     b_send.at[it, g, step], b_recv.at[it, g, step], row=row,
                 ).wait_recv()
-                total = total + rowbuf[it, g, step]
-            url_labels = total * udeg_inv[0:1, :]
+                total = total + decode(rowbuf.at[it, g, step], u_local)
+            url_labels = total
             if it == ITERS - 1:
                 url_out[g * members:(g + 1) * members, :] = url_labels
             mine = place(ugrid[it][g], row, u_split, u_local)
@@ -264,18 +289,19 @@
                     dsend[it, g, owner] = scaled
             for step in range(1, n_col):
                 peer = lax.rem(col + step, n_col)
+                encode(dcode.at[it, g, step], dsend[it, g, peer])
                 go(copy(
-                    dsend.at[it, g, peer], drecv.at[it, g, step],
+                    dcode.at[it, g, step], drecv.at[it, g, step],
                     d_send.at[it, g, step], d_recv.at[it, g, step], col=peer,
                 ))
             yield
             total = dsend[it, g, col]
             for step in range(1, n_col):
                 copy(
-                    dsend.at[it, g, step], drecv.at[it, g, step],
+                    dcode.at[it, g, step], drecv.at[it, g, step],
                     d_send.at[it, g, step], d_recv.at[it, g, step], col=col,
                 ).wait_recv()
-                total = total + drecv[it, g, step]
+                total = total + decode(drecv.at[it, g, step], q_local)
             rows = slice(g * members, (g + 1) * members)
             labels = total + seeds[rows, :]
             if it == ITERS - 1:
@@ -285,14 +311,14 @@
                 start_queries(it + 1, g)
         yield
 
-    stages = 6 * ITERS
     flows = [flow(g) for g in range(groups)]
     for g in range(groups):
         next(flows[g])
-    for slot in range(stages + SKEW * (groups - 1)):
-        for g in range(groups):
-            if 0 <= slot - SKEW * g < stages:
-                next(flows[g])
+    for it in range(ITERS):
+        for stages in ((0,), (1,), (2,), (3, 4), (5,)):
+            for g in range(groups):
+                for stage in stages:
+                    next(flows[g])
     for op in started:
         op.wait_send()
 
@@ -316,16 +342,18 @@
         [[pltpu.VMEM((q_blocks, members, side), bf16)] * groups] * ITERS,
         pltpu.VMEM(lead + (2, chips, members, u_local), f32),
         pltpu.VMEM(lead + (chips, members, u_local), f32),
-        pltpu.VMEM(lead + (chips, members, u_local), f32),
-        pltpu.VMEM(lead + (chips, members, u_local), f32),
+        pltpu.VMEM(lead + (chips, members, u_local + SCALE_LANES), jnp.int16),
+        pltpu.VMEM(lead + (chips, members, u_local + SCALE_LANES), jnp.int16),
+        pltpu.VMEM(lead + (members, u_local), f32),
         [[pltpu.VMEM((BC, members, side), bf16)] * groups] * ITERS,
         pltpu.VMEM(lead + (n_col, members, q_local), f32),
-        pltpu.VMEM(lead + (n_col, members, q_local), f32),
-        pltpu.VMEM((n_row, 8, u_local), f32),
-        pltpu.VMEM((n_row, 8, u_local), f32),
+        pltpu.VMEM(lead + (n_col, members, q_local + SCALE_LANES), jnp.int16),
+        pltpu.VMEM(lead + (n_col, members, q_local + SCALE_LANES), jnp.int16),
+        pltpu.VMEM((n_row, u_local), f32),
+        pltpu.VMEM((n_row, n_row, u_local), f32),
         pltpu.VMEM((max(n_col, 8), q_local), f32),
         pltpu.VMEM((n_col, max(n_col, 8), q_local), f32),
-        pltpu.VMEM((8, u_local), f32),
+        pltpu.VMEM((n_row, 8, u_local), f32),
         pltpu.VMEM((max(n_col, 8), q_local), f32),
         pltpu.VMEM((classes, q_local), f32),
         pltpu.SMEM((2, slots), jnp.int32),
@@ -356,7 +384,7 @@
         out_specs=(vmem, vmem),
         scratch_shapes=scratch,
         compiler_params=pltpu.CompilerParams(
-            collective_id=0, has_side_effects=True, vmem_limit_bytes=60 * 1024 * 1024
+            collective_id=0, has_side_effects=True, vmem_limit_bytes=56 * 1024 * 1024
         ),
     )(tile_coords.T, tile_count[None, :], prior_labels, seed_ids[None, :], seed_class[None, :], click_tiles)
 

time: 77.9 us -> 67.2 us (0.86)
  Pallas kernels: 73.3 us -> 62.6 us
    pallas_call x1, Pallas kernels: 73.3 us -> 62.6 us  [shards(): pl.pallas_call(functools.partial(kernel, n_row, n_col), out_shape=(jax.Sh...]
where the time goes in v4:
time: 67.2 us; the launch traced here: 67 us
  Pallas kernels  62.6 us (93%)
  local copies, waits for them, and re-layouts  3.14 us (5%)
  between operations  1.28 us (2%)
    pallas_call x1, Pallas kernels, shards(): pl.pallas_call(functools.partial(kernel, n_row, n_col), out_shape=(jax.Sh...  62.6 us
    unnamed x2, local copies, waits for them, and re-layouts  3.14 us

profile of v4, /device:TPU:0, one launch (start us, length us, event | category | flops | bytes accessed | tf_op | source)
XLA Modules:
  0.0 67.0 jit_solution(9396317433337469795)
XLA Ops:
  1.3 62.6 %shard_map.77 = (f32[64,512]{1,0:T(8,128)}, f32[64,512]{1,0:T(8,128)}) custom-call(s32[2,8]{1,0:T(2,128)} %bitcast.5, s32[1,1]{1,0:T(1,128)} %bitcast.4.count_hbm, f32[64,512]{1,0:T(8,128)} %prior_hbm.1, s32[1,32]{1,0:T(1,128)} %bitcast.6, s32[1,32]{1,0:T(1,128)} %bitcast.7, bf16[8,512,512]{2,1,0:T(8,128)(2,1)} %tiles_hbm.1), custom_call_target="tpu_custom_call" | custom-call | tf_op jit(solution)/shard_map/pallas_call | solution.py:377
  63.9 1.6 %copy.11 = f32[64,512]{1,0:T(8,128)} copy(f32[64,512]{1,0:T(8,128)} %get-tuple-element.4) | data formatting | bytes 262144
  65.5 1.6 %copy.12 = f32[64,512]{1,0:T(8,128)} copy(f32[64,512]{1,0:T(8,128)} %get-tuple-element.5) | data formatting | bytes 262144

commit v5 on v4

--- a/solution.py
+++ b/solution.py
@@ -9,7 +9,7 @@
 
 BC = 8
 ITERS = 2
-GROUPS = 2
+GROUPS = 4
 WIRE_TOP = 32767.0
 SCALE_LANES = 128
 SCALE_STEPS = 256.0
@@ -311,14 +311,14 @@
                 start_queries(it + 1, g)
         yield
 
+    stages = 6 * ITERS
     flows = [flow(g) for g in range(groups)]
     for g in range(groups):
         next(flows[g])
-    for it in range(ITERS):
-        for stages in ((0,), (1,), (2,), (3, 4), (5,)):
-            for g in range(groups):
-                for stage in stages:
-                    next(flows[g])
+    for slot in range(stages + groups - 1):
+        for g in range(groups):
+            if 0 <= slot - g < stages:
+                next(flows[g])
     for op in started:
         op.wait_send()
 

time: 67.2 us -> 77.2 us (1.15)
  Pallas kernels: 62.6 us -> 72.6 us
    pallas_call x1, Pallas kernels: 62.6 us -> 72.6 us  [shards(): pl.pallas_call(functools.partial(kernel, n_row, n_col), out_shape=(jax.Sh...]
where the time goes in v5:
time: 77.2 us; the launch traced here: 77 us
  Pallas kernels  72.6 us (94%)
  local copies, waits for them, and re-layouts  3.14 us (4%)
  between operations  1.28 us (2%)
    pallas_call x1, Pallas kernels, shards(): pl.pallas_call(functools.partial(kernel, n_row, n_col), out_shape=(jax.Sh...  72.6 us
    unnamed x2, local copies, waits for them, and re-layouts  3.14 us

profile of v5, /device:TPU:0, one launch (start us, length us, event | category | flops | bytes accessed | tf_op | source)
XLA Modules:
  0.0 77.0 jit_solution(15247422275890137409)
XLA Ops:
  1.3 72.6 %shard_map.77 = (f32[64,512]{1,0:T(8,128)}, f32[64,512]{1,0:T(8,128)}) custom-call(s32[2,8]{1,0:T(2,128)} %bitcast.5, s32[1,1]{1,0:T(1,128)} %bitcast.4.count_hbm, f32[64,512]{1,0:T(8,128)} %prior_hbm.1, s32[1,32]{1,0:T(1,128)} %bitcast.6, s32[1,32]{1,0:T(1,128)} %bitcast.7, bf16[8,512,512]{2,1,0:T(8,128)(2,1)} %tiles_hbm.1), custom_call_target="tpu_custom_call" | custom-call | tf_op jit(solution)/shard_map/pallas_call | solution.py:377
  73.8 1.6 %copy.11 = f32[64,512]{1,0:T(8,128)} copy(f32[64,512]{1,0:T(8,128)} %get-tuple-element.4) | data formatting | bytes 262144
  75.4 1.6 %copy.12 = f32[64,512]{1,0:T(8,128)} copy(f32[64,512]{1,0:T(8,128)} %get-tuple-element.5) | data formatting | bytes 262144

commit v6 on v4

--- a/solution.py
+++ b/solution.py
@@ -9,7 +9,7 @@
 
 BC = 8
 ITERS = 2
-GROUPS = 2
+GROUPS = 1
 WIRE_TOP = 32767.0
 SCALE_LANES = 128
 SCALE_STEPS = 256.0

time: 67.2 us -> 74.8 us (1.11)
  Pallas kernels: 62.6 us -> 70.2 us
    pallas_call x1, Pallas kernels: 62.6 us -> 70.2 us  [shards(): pl.pallas_call(functools.partial(kernel, n_row, n_col), out_shape=(jax.Sh...]
where the time goes in v6:
time: 74.8 us; the launch traced here: 74.6 us
  Pallas kernels  70.2 us (94%)
  local copies, waits for them, and re-layouts  3.14 us (4%)
  between operations  1.28 us (2%)
    pallas_call x1, Pallas kernels, shards(): pl.pallas_call(functools.partial(kernel, n_row, n_col), out_shape=(jax.Sh...  70.2 us
    unnamed x2, local copies, waits for them, and re-layouts  3.14 us

profile of v6, /device:TPU:0, one launch (start us, length us, event | category | flops | bytes accessed | tf_op | source)
XLA Modules:
  0.0 74.6 jit_solution(692368546739989739)
XLA Ops:
  1.3 70.2 %shard_map.77 = (f32[64,512]{1,0:T(8,128)}, f32[64,512]{1,0:T(8,128)}) custom-call(s32[2,8]{1,0:T(2,128)} %bitcast.5, s32[1,1]{1,0:T(1,128)} %bitcast.4.count_hbm, f32[64,512]{1,0:T(8,128)} %prior_hbm.1, s32[1,32]{1,0:T(1,128)} %bitcast.6, s32[1,32]{1,0:T(1,128)} %bitcast.7, bf16[8,512,512]{2,1,0:T(8,128)(2,1)} %tiles_hbm.1), custom_call_target="tpu_custom_call" | custom-call | tf_op jit(solution)/shard_map/pallas_call | solution.py:377
  71.5 1.6 %copy.11 = f32[64,512]{1,0:T(8,128)} copy(f32[64,512]{1,0:T(8,128)} %get-tuple-element.4) | data formatting | bytes 262144
  73.1 1.6 %copy.12 = f32[64,512]{1,0:T(8,128)} copy(f32[64,512]{1,0:T(8,128)} %get-tuple-element.5) | data formatting | bytes 262144
